TPU v7x, 32 devices: a whole 2x2x4 slice. The times are simulated.
32 devices in a mesh: dp: 16 (over z, y, core), tensor: 2 (over x).
Axes of the slice: x: 2, y: 2, z: 4, core: 2. Of those that a mesh axis runs over, the one named last changes fastest.
Arguments:
- inputs: bfloat16 [16384, 1024], P(('dp', 'tensor')), may hold values from -6 to 6
- segment_ids: int32 [16384], P('dp'), may hold values from 0 to 1023, as said below
- ln_attn_gain: bfloat16 [1024], P(('dp', 'tensor')), may hold values from 0.25 to 1.75
- ln_attn_bias: bfloat16 [1024], P(('dp', 'tensor')), may hold values from -1.75 to 1.75
- ln_mlp_gain: bfloat16 [1024], P(('dp', 'tensor')), may hold values from 0.25 to 1.75
- ln_mlp_bias: bfloat16 [1024], P(('dp', 'tensor')), may hold values from -1.75 to 1.75
- qkv_weight: bfloat16 [1024, 3, 1024], P('dp', None, 'tensor'), may hold values from -0.1875 to 0.1875
- qkv_bias: bfloat16 [3, 2, 512], P(None, 'tensor', 'dp'), may hold values from -3 to 3
- out_weight: bfloat16 [1024, 1024], P('tensor', 'dp'), may hold values from -2 to 2
- out_bias: bfloat16 [1024], P(('dp', 'tensor')), may hold values from -1.75 to 1.75
- up_weight: bfloat16 [1024, 4096], P('dp', 'tensor'), may hold values from -0.1875 to 0.1875
- up_bias: bfloat16 [2, 2048], P('tensor', 'dp'), may hold values from -3 to 3
- down_weight: bfloat16 [4096, 1024], P('tensor', 'dp'), may hold values from -0.09375 to 0.09375
- down_bias: bfloat16 [1024], P(('dp', 'tensor')), may hold values from -1.75 to 1.75
- cotangent: bfloat16 [16384, 1024], P(('dp', 'tensor')), may hold values from -6 to 6
Outputs:
- output: bfloat16 [16384, 1024], P(('dp', 'tensor'))
- input_grad: float32 [16384, 1024], P(('dp', 'tensor'))
- d_ln_attn_gain: float32 [1024], P(('dp', 'tensor'))
- d_ln_attn_bias: float32 [1024], P(('dp', 'tensor'))
- d_ln_mlp_gain: float32 [1024], P(('dp', 'tensor'))
- d_ln_mlp_bias: float32 [1024], P(('dp', 'tensor'))
- d_qkv_weight: float32 [1024, 3, 1024], P('dp', None, 'tensor')
- d_qkv_bias: float32 [3, 2, 512], P(None, 'tensor', 'dp')
- d_out_weight: float32 [1024, 1024], P('tensor', 'dp')
- d_out_bias: float32 [1024], P(('dp', 'tensor'))
- d_up_weight: float32 [1024, 4096], P('dp', 'tensor')
- d_up_bias: float32 [2, 2048], P('tensor', 'dp')
- d_down_weight: float32 [4096, 1024], P('tensor', 'dp')
- d_down_bias: float32 [1024], P(('dp', 'tensor'))
Inputs may be any that keep to these rules, and one draw needn't show every extreme that they name: `segment_ids`: within each packed sequence of 1024 tokens a token's number is the position, within that sequence, of its document's first token, so the numbers never fall and a run of equal numbers is one document; the last token of each sequence is a document of its own.
All inputs are finite; a program needn't handle non-finite values.
Results may differ from a plain program's by a relative error of at most 0.0098.
Values may be sent and summed in bfloat16 or wider, within the bound.
A program may use at most 256 MiB of HBM per device.

v0:
```python
import math

import jax
import jax.numpy as jnp
from jax import lax
from jax.sharding import PartitionSpec as P

HEAD = 64
ROT = 16


EPSILON = 1e-05
NEGATIVE = -1e30


def rotated(values, cosine, sine, sign):
    half_rot = ROT // 2
    first_half = values[..., :half_rot]
    second_half = values[..., half_rot:ROT]
    new_first = first_half * cosine - sign * second_half * sine
    new_second = second_half * cosine + sign * first_half * sine
    return jnp.concatenate([new_first, new_second, values[..., ROT:]], axis=-1)


def angle_tables(length):
    position = jnp.arange(length).astype(jnp.float32)
    inverse = 10000.0 ** (-(2.0 * jnp.arange(ROT // 2).astype(jnp.float32)) / ROT)
    theta = position[:, None] * inverse[None, :]
    return (jnp.cos(theta)[:, None, :], jnp.sin(theta)[:, None, :])


def gelu_exact(value):
    return jax.nn.gelu(value, approximate=False)


def layer_norm(rows):
    centred = rows - jnp.mean(rows, axis=-1, keepdims=True)
    inv_std = lax.rsqrt(jnp.mean(centred * centred, axis=-1, keepdims=True) + EPSILON)
    return (centred * inv_std, inv_std)


def local(
    inputs,
    segment_ids,
    ln_attn_gain,
    ln_attn_bias,
    ln_mlp_gain,
    ln_mlp_bias,
    qkv_weight,
    qkv_bias,
    out_weight,
    out_bias,
    up_weight,
    up_bias,
    down_weight,
    down_bias,
    cotangent,
):
    seq_len = segment_ids.shape[0]
    norm_terms = (
        lax.all_gather(ln_attn_gain, ("dp", "tensor"), axis=0, tiled=True),
        lax.all_gather(ln_attn_bias, ("dp", "tensor"), axis=0, tiled=True),
        lax.all_gather(ln_mlp_gain, ("dp", "tensor"), axis=0, tiled=True),
        lax.all_gather(ln_mlp_bias, ("dp", "tensor"), axis=0, tiled=True),
        lax.all_gather(out_bias, ("dp", "tensor"), axis=0, tiled=True),
        lax.all_gather(down_bias, ("dp", "tensor"), axis=0, tiled=True),
    )
    gain_attn = norm_terms[0].astype(jnp.float32)
    shift_attn = norm_terms[1].astype(jnp.float32)
    gain_mlp = norm_terms[2].astype(jnp.float32)
    shift_mlp = norm_terms[3].astype(jnp.float32)
    bias_sum = norm_terms[4].astype(jnp.float32) + norm_terms[5].astype(jnp.float32)
    w_qkv, b_qkv, w_out, w_up, b_up, w_down = (
        lax.all_gather(qkv_weight, "dp", axis=0, tiled=True),
        lax.all_gather(qkv_bias, "dp", axis=2, tiled=True),
        lax.all_gather(out_weight, "dp", axis=1, tiled=True),
        lax.all_gather(up_weight, "dp", axis=0, tiled=True),
        lax.all_gather(up_bias, "dp", axis=1, tiled=True),
        lax.all_gather(down_weight, "dp", axis=1, tiled=True),
    )
    local_width = w_qkv.shape[2]
    heads_here = local_width // HEAD
    score_scale = 1.0 / math.sqrt(HEAD)
    resid = inputs.astype(jnp.float32)
    normalized, inv_std = layer_norm(resid)
    whole_inputs = lax.all_gather(inputs, "tensor", axis=0, tiled=True)
    normal_all, unused_std = layer_norm(whole_inputs.astype(jnp.float32))
    attn_rows = (normal_all * gain_attn + shift_attn).astype(jnp.bfloat16)
    mlp_rows = (normal_all * gain_mlp + shift_mlp).astype(jnp.bfloat16)
    proj = jnp.einsum("sd,dje->sje", attn_rows, w_qkv, preferred_element_type=jnp.float32)
    proj = proj + b_qkv.astype(jnp.float32).reshape(1, 3, local_width)
    cosine, sine = angle_tables(seq_len)
    query = rotated(proj[:, 0].reshape(seq_len, heads_here, HEAD), cosine, sine, 1.0).astype(
        jnp.bfloat16
    )
    keys = rotated(proj[:, 1].reshape(seq_len, heads_here, HEAD), cosine, sine, 1.0).astype(
        jnp.bfloat16
    )
    values = proj[:, 2].reshape(seq_len, heads_here, HEAD).astype(jnp.bfloat16)
    block_rows = min(512, seq_len)
    block_count = seq_len // block_rows
    places = jnp.arange(seq_len)
    query_blocks = query.reshape(block_count, block_rows, heads_here, HEAD)
    segment_blocks = segment_ids.reshape(block_count, block_rows)
    place_blocks = places.reshape(block_count, block_rows)

    def masked_scores(query_part, segment_part, place_part):
        scores = (
            jnp.einsum("qhe,khe->hqk", query_part, keys, preferred_element_type=jnp.float32)
            * score_scale
        )
        allowed = (segment_part[:, None] == segment_ids[None, :]) & (
            place_part[:, None] >= places[None, :]
        )
        return jnp.where(allowed[None], scores, NEGATIVE)

    def forward_block(block_item):
        query_part, segment_part, place_part = block_item
        scores = masked_scores(query_part, segment_part, place_part)
        row_max = jnp.max(scores, axis=-1, keepdims=True)
        exponent = jnp.exp(scores - row_max)
        row_total = jnp.sum(exponent, axis=-1, keepdims=True)
        probability = (exponent / row_total).astype(jnp.bfloat16)
        context_part = jnp.einsum(
            "hqk,khe->qhe", probability, values, preferred_element_type=jnp.float32
        )
        return (context_part, (row_max + jnp.log(row_total))[..., 0])

    context_blocks, log_totals = lax.map(
        forward_block, (query_blocks, segment_blocks, place_blocks)
    )
    context = context_blocks.reshape(seq_len, local_width).astype(jnp.bfloat16)
    up_in = jnp.dot(mlp_rows, w_up, preferred_element_type=jnp.float32) + b_up.astype(jnp.float32)
    activated = gelu_exact(up_in).astype(jnp.bfloat16)
    context_part = context
    branch_sum = lax.psum_scatter(
        jnp.dot(context_part, w_out, preferred_element_type=jnp.float32)
        + jnp.dot(activated, w_down, preferred_element_type=jnp.float32),
        "tensor",
        scatter_dimension=0,
        tiled=True,
    )
    output = (resid + branch_sum + bias_sum).astype(jnp.bfloat16)
    grad_all = lax.all_gather(cotangent, "tensor", axis=0, tiled=True)
    d_active = jnp.einsum("sd,fd->sf", grad_all, w_down, preferred_element_type=jnp.float32)
    gelu_value, gelu_back = jax.vjp(gelu_exact, up_in)
    d_up = gelu_back(d_active)[0].astype(jnp.bfloat16)
    d_w_down = jnp.einsum("sf,sd->fd", activated, grad_all, preferred_element_type=jnp.float32)
    d_w_up = jnp.einsum("sd,sf->df", mlp_rows, d_up, preferred_element_type=jnp.float32)
    d_b_up = jnp.sum(d_up, axis=0, dtype=jnp.float32).reshape(1, -1)
    unit_sums = (d_w_up, d_b_up, d_w_down)
    d_context = jnp.einsum("sd,cd->sc", grad_all, w_out, preferred_element_type=jnp.float32).astype(
        jnp.bfloat16
    )
    d_w_out = jnp.einsum("sc,sd->cd", context, grad_all, preferred_element_type=jnp.float32)
    d_context_blocks = d_context.reshape(block_count, block_rows, heads_here, HEAD)

    def backward_block(carry, block_item):
        d_keys, d_values = carry
        query_part, d_context_part, segment_part, place_part, log_part = block_item
        scores = masked_scores(query_part, segment_part, place_part)
        probability = jnp.exp(scores - log_part[..., None])
        d_prob = jnp.einsum(
            "qhe,khe->hqk", d_context_part, values, preferred_element_type=jnp.float32
        )
        row_delta = jnp.sum(probability * d_prob, axis=-1, keepdims=True)
        d_scores = (probability * (d_prob - row_delta)).astype(jnp.bfloat16)
        d_query_part = (
            jnp.einsum("hqk,khe->qhe", d_scores, keys, preferred_element_type=jnp.float32)
            * score_scale
        )
        d_keys = (
            d_keys
            + jnp.einsum("hqk,qhe->khe", d_scores, query_part, preferred_element_type=jnp.float32)
            * score_scale
        )
        d_values = d_values + jnp.einsum(
            "hqk,qhe->khe",
            probability.astype(jnp.bfloat16),
            d_context_part,
            preferred_element_type=jnp.float32,
        )
        return ((d_keys, d_values), d_query_part)

    zero_rows = jnp.zeros((seq_len, heads_here, HEAD), jnp.float32)
    (d_keys, d_values), d_query_blocks = lax.scan(
        backward_block,
        (zero_rows, zero_rows),
        (query_blocks, d_context_blocks, segment_blocks, place_blocks, log_totals),
    )
    d_query = d_query_blocks.reshape(seq_len, heads_here, HEAD)
    d_proj = jnp.stack(
        [
            rotated(d_query, cosine, sine, -1.0).reshape(seq_len, local_width),
            rotated(d_keys, cosine, sine, -1.0).reshape(seq_len, local_width),
            d_values.reshape(seq_len, local_width),
        ],
        axis=1,
    ).astype(jnp.bfloat16)
    d_w_qkv = jnp.einsum("sd,sje->dje", attn_rows, d_proj, preferred_element_type=jnp.float32)
    d_b_qkv = jnp.sum(d_proj, axis=0, dtype=jnp.float32).reshape(3, 1, local_width)
    grad_rows = cotangent.astype(jnp.float32)
    attn_term = jnp.einsum("sje,dje->sd", d_proj, w_qkv, preferred_element_type=jnp.float32)
    mlp_term = jnp.einsum("sf,df->sd", d_up, w_up, preferred_element_type=jnp.float32)
    stacked = lax.psum_scatter(
        jnp.stack([attn_term, mlp_term], axis=1), "tensor", scatter_dimension=0, tiled=True
    )
    d_attn_norm = stacked[:, 0]
    d_mlp_norm = stacked[:, 1]
    d_hat = d_attn_norm * gain_attn + d_mlp_norm * gain_mlp
    norm_sums = (
        jnp.sum(d_attn_norm * normalized, axis=0),
        jnp.sum(d_attn_norm, axis=0),
        jnp.sum(d_mlp_norm * normalized, axis=0),
        jnp.sum(d_mlp_norm, axis=0),
    )
    input_grad = grad_rows + inv_std * (
        d_hat
        - jnp.mean(d_hat, axis=-1, keepdims=True)
        - normalized * jnp.mean(d_hat * normalized, axis=-1, keepdims=True)
    )
    small_sums = (
        lax.psum_scatter(norm_sums[0], ("dp", "tensor"), scatter_dimension=0, tiled=True),
        lax.psum_scatter(norm_sums[1], ("dp", "tensor"), scatter_dimension=0, tiled=True),
        lax.psum_scatter(norm_sums[2], ("dp", "tensor"), scatter_dimension=0, tiled=True),
        lax.psum_scatter(norm_sums[3], ("dp", "tensor"), scatter_dimension=0, tiled=True),
        lax.psum_scatter(
            jnp.sum(grad_rows, axis=0), ("dp", "tensor"), scatter_dimension=0, tiled=True
        ),
    )
    summed = (
        lax.psum_scatter(d_w_qkv, "dp", scatter_dimension=0, tiled=True),
        lax.psum_scatter(d_b_qkv, "dp", scatter_dimension=2, tiled=True),
        lax.psum_scatter(d_w_out, "dp", scatter_dimension=1, tiled=True),
        lax.psum_scatter(unit_sums[0], "dp", scatter_dimension=0, tiled=True),
        lax.psum_scatter(unit_sums[1], "dp", scatter_dimension=1, tiled=True),
        lax.psum_scatter(unit_sums[2], "dp", scatter_dimension=1, tiled=True),
    )
    return (
        output,
        input_grad,
        small_sums[0],
        small_sums[1],
        small_sums[2],
        small_sums[3],
        summed[0],
        summed[1],
        summed[2],
        small_sums[4],
        summed[3],
        summed[4],
        summed[5],
        small_sums[4],
    )


def solution(mesh):
    return jax.shard_map(
        local,
        mesh=mesh,
        in_specs=(
            P(("dp", "tensor"), None),
            P("dp"),
            P(("dp", "tensor")),
            P(("dp", "tensor")),
            P(("dp", "tensor")),
            P(("dp", "tensor")),
            P("dp", None, "tensor"),
            P(None, "tensor", "dp"),
            P("tensor", "dp"),
            P(("dp", "tensor")),
            P("dp", "tensor"),
            P("tensor", "dp"),
            P("tensor", "dp"),
            P(("dp", "tensor")),
            P(("dp", "tensor"), None),
        ),
        out_specs=(
            P(("dp", "tensor"), None),
            P(("dp", "tensor"), None),
            P(("dp", "tensor")),
            P(("dp", "tensor")),
            P(("dp", "tensor")),
            P(("dp", "tensor")),
            P("dp", None, "tensor"),
            P(None, "tensor", "dp"),
            P("tensor", "dp"),
            P(("dp", "tensor")),
            P("dp", "tensor"),
            P("tensor", "dp"),
            P("tensor", "dp"),
            P(("dp", "tensor")),
        ),
        check_vma=False,
    )
```

profile of v0, /device:TPU:0, one launch (start us, length us, event | category | flops | bytes accessed | tf_op | source)
XLA Modules:
  0.0 1019.4 jit_solution(15780108305444164989)
XLA Ops:
  16.3 42.4 %all-reduce.12 = (bf16[1024]{0:T(1024)(128)(2,1)S(1)}, bf16[1024]{0:T(1024)(128)(2,1)S(1)}, bf16[1024]{0:T(1024)(128)(2,1)S(1)}, bf16[1024]{0:T(1024)(128)(2,1)S...) all-reduce(bf16[1024]{0:T(1024)(128)(2,1)S(1)} %dynamic-update-slic, ...), channel_id=1, replica_groups=mesh['dp'=16,'tensor'=2] {'dp','tensor'}, use_global_device_ids=true, to_apply=%add.3 | all-reduce | flops 6144 | bytes 24576
  59.5 22.6 %all_gather.46 = bf16[3,1,512]{0,1,2:T(2,128)(2,1)S(1)} all-gather(bf16[3,1,32]{0,1,2:T(2,128)(2,1)S(1)} %copy.48), channel_id=1, replica_groups=mesh['dp'=16,'tensor'=2] {'dp'}, dimensions={2}, use_global_device_ids=true | all-gather | bytes 3264 | tf_op jit(solution)/shard_map/all_gather | solution.py:75
  84.5 17.5 %all_gather.51 = bf16[1,2048]{1,0:T(2,128)(2,1)S(1)} all-gather(bf16[1,128]{1,0:T(2,128)(2,1)} %param.30), channel_id=1, replica_groups=mesh['dp'=16,'tensor'=2] {'dp'}, dimensions={1}, use_global_device_ids=true | all-gather | bytes 4352 | tf_op jit(solution)/shard_map/all_gather | solution.py:78
  107.7 12.8 %all-gather.17.cloned.1.call-done = bf16[1024,1024]{1,0:T(8,128)(2,1)} async-done(((bf16[512,1024]{1,0:T(8,128)(2,1)}), bf16[1024,1024]{1,0:T(8,128)(2,1)}) %all-gather.17.cloned.1.call-update) | async-done | bytes 2097168 | tf_op jit(solution)/shard_map/all_gather | solution.py:144
  126.9 40.8 %all-gather.9.cloned.1.call-done = bf16[1024,3,512]{2,0,1:T(8,128)(2,1)} async-done(((bf16[64,3,512]{2,0,1:T(8,128)(2,1)}), bf16[1024,3,512]{2,0,1:T(8,128)(2,1)}) %all-gather.9.cloned.1.call-update) | async-done | bytes 3145744 | tf_op jit(solution)/shard_map/all_gather | solution.py:74
  167.8 6.4 broadcast_add_fusion
  178.5 31.4 %while.28 = (s32[]{:T(128)}, bf16[2,512,8,64]{1,3,2,0:T(8,128)(2,1)S(1)}, f32[2,8,512]{2,1,0:T(8,128)}, s32[2,512]{1,0:T(2,128)S(1)}, s32[1024]{0:T(1024)S(1)}, ...) while((s32[]{:T(128)}, ...), condition=%wide.region_5.6_spmd.clone, body=%wide.region_2.5_spmd.clone.sunk | while | flops 1125642240 | bytes 56247404 | solution.py:129
  179.3 4.1 fusion.126
  183.4 4.2 fusion.127
  188.3 5.9 fusion.128
  194.8 4.3 fusion.126
  199.1 4.2 fusion.127
  203.9 5.9 fusion.128
  210.8 140.9 %while.29 = (s32[]{:T(128)}, f32[1024,8,64]{0,2,1:T(8,128)}, f32[1024,8,64]{0,2,1:T(8,128)}, f32[2,512,8,64]{1,0,3,2:T(2,128)}, bf16[2,512,8,64]{1,3,2,0:T(8,128...) while((s32[]{:T(128)}, f32[1024,8,64]{0,2,1:T(8,128)}, ...), condition=%wide.region_11.12_spmd.clone, body=%wide.region_9.11_spmd.clone.sunk | while | flops 2726555648 | bytes 166823680 | solution.py:186
  212.6 3.8 fusion.138
  217.7 11.4 %multiply_reduce_fusion.2 = (f32[8,512]{1,0:T(8,128)}, f32[8,512,1024]{2,1,0:T(8,128)}) fusion(f32[8,512,1024]{2,1,0:T(8,128)S(1)} %fusion.138, f32[8,512]{1,0:T(8,128)} %dynamic-slice_bitcast_fusion.2, bf16[1024,8,64]{0,2,1:T(8,128)(2,1)S(1)} %get-tuple-element.543, bf16[2,512,8,64]{1,3,2,0:T(8,128)(2,1)} %get-tuple-element.539, ...), kind=kOutput, calls=%fused_computation.22.clone.1 | convolution fusion | flops 557838336 | bytes 35684864 | tf_op jit(solution)/shard_map/while/body/eval_jaxpr/qhe,khe->hqk/dot_general | solution.py:109
  229.1 9.3 multiply_convert_fusion.3
  238.4 6.1 fusion.140
  246.6 19.6 %dynamic_update_slice.21 = f32[2,512,8,64]{1,0,3,2:T(2,128)} dynamic-update-slice(f32[2,512,8,64]{1,0,3,2:T(2,128)} %get-tuple-element.524, f32[1,512,8,64]{1,0,3,2:T(1,128)} %copy.90, s32[]{:T(128)} %get-tuple-element.521, s32[]{:T(128)} %constant.64.clone.1..sunk, s32[]{:T(128)} %constant.64.clone.1..sunk, s32[]{:T(128)} %constant.64.clone.1..sunk) | dynamic-update-slice | bytes 2097156 | tf_op jit(solution)/shard_map/while/body/jit(dynamic_update_index_in_dim)/dynamic_update_slice | solution.py:129
  266.2 5.6 bitcast_add_fusion.4
  271.9 9.4 bitcast_add_fusion.5
  282.7 3.8 fusion.138
  287.7 11.4 %multiply_reduce_fusion.2 = (f32[8,512]{1,0:T(8,128)}, f32[8,512,1024]{2,1,0:T(8,128)}) fusion(f32[8,512,1024]{2,1,0:T(8,128)S(1)} %fusion.138, f32[8,512]{1,0:T(8,128)} %dynamic-slice_bitcast_fusion.2, bf16[1024,8,64]{0,2,1:T(8,128)(2,1)S(1)} %get-tuple-element.543, bf16[2,512,8,64]{1,3,2,0:T(8,128)(2,1)} %get-tuple-element.539, ...), kind=kOutput, calls=%fused_computation.22.clone.1 | convolution fusion | flops 557838336 | bytes 35684864 | tf_op jit(solution)/shard_map/while/body/eval_jaxpr/qhe,khe->hqk/dot_general | solution.py:109
  299.2 9.3 multiply_convert_fusion.3
  308.5 6.1 fusion.140
  316.6 19.6 %dynamic_update_slice.21 = f32[2,512,8,64]{1,0,3,2:T(2,128)} dynamic-update-slice(f32[2,512,8,64]{1,0,3,2:T(2,128)} %get-tuple-element.524, f32[1,512,8,64]{1,0,3,2:T(1,128)} %copy.90, s32[]{:T(128)} %get-tuple-element.521, s32[]{:T(128)} %constant.64.clone.1..sunk, s32[]{:T(128)} %constant.64.clone.1..sunk, s32[]{:T(128)} %constant.64.clone.1..sunk) | dynamic-update-slice | bytes 2097156 | tf_op jit(solution)/shard_map/while/body/jit(dynamic_update_index_in_dim)/dynamic_update_slice | solution.py:129
  336.3 5.4 bitcast_add_fusion.4
  341.7 10.0 bitcast_add_fusion.5
  351.7 4.3 reshape.315
  367.1 8.0 convolution_bitcast_fusion.1
  375.2 9.3 fusion.71
  384.5 27.9 %convert_reduce_fusion = (f32[2048]{0:T(1024)S(1)}, bf16[1024,2048]{1,0:T(8,128)(2,1)}, f32[1024,2048]{1,0:T(8,128)}) fusion(f32[1024,2048]{1,0:T(8,128)} %fusion.71, f32[2048]{0:T(1024)S(1)} %bitcast.177, bf16[1024,1024]{1,0:T(8,128)(2,1)} %all-gather.17.cloned.1.call-done, bf16[2048,1024]{0,1:T(8,128)(2,1)} %all-gather.15.cloned.1.call-done), kind=kOutput, calls=%fused_computation.51 | convolution fusion | flops 4452251648 | bytes 27279360 | tf_op jit(solution)/shard_map/sd,fd->sf/dot_general | solution.py:145
  413.9 7.8 convolution_bitcast_fusion
  421.7 4.1 pad_maximum_fusion
  428.8 10.7 %multiply_convert_fusion.1 = bf16[1024,2048]{1,0:T(8,128)(2,1)} fusion(f32[1024,2048]{1,0:T(8,128)} %get-tuple-element.301, f32[1024,2048]{1,0:T(8,128)} %fusion.71, f32[2048]{0:T(1024)S(1)} %bitcast.178), kind=kLoop, calls=%fused_computation.53 | loop fusion | flops 8388608 | bytes 20979712 | tf_op jit(solution)/shard_map/convert_element_type | solution.py:134
  439.5 7.8 fusion.77
  450.7 4.6 fusion.78
  455.4 7.9 fusion.66
  463.6 10.7 %fusion.79 = f32[2048,1024]{0,1:T(8,128)} fusion(bf16[1024,2048]{1,0:T(8,128)(2,1)} %multiply_convert_fusion.1, bf16[1024,1024]{1,0:T(8,128)(2,1)} %all-gather.17.cloned.1.call-done), kind=kOutput, calls=%fused_computation.151 | convolution fusion | flops 4294967296 | bytes 14680064 | tf_op jit(solution)/shard_map/sf,sd->fd/dot_general | solution.py:148
  474.4 9.3 fusion.69
  488.6 93.6 %reduce-scatter.15.cloned.1.call-done = f32[512,2,1024]{2,0,1:T(8,128)} async-done(((f32[1024,2,1024]{2,0,1:T(8,128)}), f32[512,2,1024]{2,0,1:T(8,128)}) %reduce-scatter.15.cloned.1.call-update) | async-done | bytes 4194320 | tf_op jit(solution)/shard_map/reduce_scatter | solution.py:205
  586.8 51.8 %reduce-scatter.13.cloned.1.call-done = f32[512,1024]{1,0:T(8,128)} async-done(((f32[1024,1024]{1,0:T(8,128)}), f32[512,1024]{1,0:T(8,128)}) %reduce-scatter.13.cloned.1.call-update) | async-done | bytes 2097168 | tf_op jit(solution)/shard_map/reduce_scatter | solution.py:136
  638.6 4.5 convert_reduce_fusion.4
  643.1 39.8 %all-reduce.11 = (f32[1024]{0:T(1024)S(1)}, f32[1024]{0:T(1024)S(1)}, f32[1024]{0:T(1024)S(1)}, f32[1024]{0:T(1024)S(1)}, f32[1024]{0:T(1024)S(1)}) all-reduce(f32[1024]{0:T(1024)S(1)} %get-tuple-element.244, f32[1024]{0:T(1024)S(1)} %get-tuple-element.241, ...), channel_id=4, replica_groups=mesh['dp'=16,'tensor'=2] {'dp','tensor'}, use_global_device_ids=true, to_apply=%region_16.17.clone | all-reduce | flops 5120 | bytes 40960
  685.3 19.9 %reduce-scatter.19.cloned.1.call-done = f32[512,64]{0,1:T(8,128)} async-done(((f32[512,1024]{0,1:T(8,128)}), f32[512,64]{0,1:T(8,128)}) %reduce-scatter.19.cloned.1.call-update) | async-done | bytes 131088 | tf_op jit(solution)/shard_map/reduce_scatter | solution.py:234
  705.2 88.6 %reduce-scatter.17.cloned.1.call-done = f32[64,3,512]{2,0,1:T(8,128)} async-done(((f32[1024,3,512]{2,0,1:T(8,128)}), f32[64,3,512]{2,0,1:T(8,128)}) %reduce-scatter.17.cloned.1.call-update) | async-done | bytes 393232 | tf_op jit(solution)/shard_map/reduce_scatter | solution.py:232
  793.8 108.9 %reduce-scatter.23.cloned.1.call-done = f32[2048,64]{0,1:T(8,128)} async-done(((f32[2048,1024]{0,1:T(8,128)}), f32[2048,64]{0,1:T(8,128)}) %reduce-scatter.23.cloned.1.call-update) | async-done | bytes 524304 | tf_op jit(solution)/shard_map/reduce_scatter | solution.py:237
  902.7 109.4 %reduce-scatter.21.cloned.1.call-done = f32[64,2048]{1,0:T(8,128)} async-done(((f32[1024,2048]{1,0:T(8,128)}), f32[64,2048]{1,0:T(8,128)}) %reduce-scatter.21.cloned.1.call-update) | async-done | bytes 524304 | tf_op jit(solution)/shard_map/reduce_scatter | solution.py:235
  (198 shorter events, 72.8 us)
Async XLA Ops:
  7.2 96.2 %all-gather.7.cloned.1.call-start = ((), (), s32[]{:S(2)}) async-start(), calls=%async_computation.8 | async-start | bytes 3145728 | tf_op jit(solution)/shard_map/all_gather | solution.py:86
  7.9 99.7 %all-gather.11.cloned.1.call-start = ((), (), s32[]{:S(2)}) async-start(), calls=%async_computation.10 | async-start | bytes 1114112 | tf_op jit(solution)/shard_map/all_gather | solution.py:76
  8.7 111.8 %all-gather.17.cloned.1.call-start = ((), (), s32[]{:S(2)}) async-start(), calls=%async_computation.14 | async-start | bytes 3145728 | tf_op jit(solution)/shard_map/all_gather | solution.py:144
  9.4 158.3 %all-gather.9.cloned.1.call-start = ((), (), s32[]{:S(2)}) async-start(), calls=%async_computation.9 | async-start | bytes 3342336 | tf_op jit(solution)/shard_map/all_gather | solution.py:74
  10.0 365.2 %all-gather.13.cloned.1.call-start = ((), (), s32[]{:S(2)}) async-start(), calls=%async_computation.11 | async-start | bytes 4456448 | tf_op jit(solution)/shard_map/all_gather | solution.py:77
  10.6 374.0 %all-gather.15.cloned.1.call-start = ((), (), s32[]{:S(2)}) async-start(), calls=%async_computation.12 | async-start | bytes 4456448 | tf_op jit(solution)/shard_map/all_gather | solution.py:79
  11.1 474.5 %reduce-scatter.25.cloned.1.call-start = ((), (), s32[]{:S(2)}) async-start(), calls=%async_computation.20 | async-start | bytes 278528
  58.7 109.0 %copy-start.19 = (f32[1024]{0:T(1024)}, f32[1024]{0:T(1024)S(1)}, u32[]{:S(2)}) copy-start(f32[1024]{0:T(1024)S(1)} %convert_element_type.152) | copy-start | bytes 12292
  58.8 109.0 %copy-start.25 = (f32[1024]{0:T(1024)}, f32[1024]{0:T(1024)S(1)}, u32[]{:S(2)}) copy-start(f32[1024]{0:T(1024)S(1)} %convert_element_type.153) | copy-start | bytes 12292
  103.4 72.6 %copy-start.15 = (f32[1024,8]{0,1:T(8,128)}, f32[1024,8]{0,1:T(8,128)S(1)}, u32[]{:S(2)}) copy-start(f32[1024,8]{0,1:T(8,128)S(1)} %get-tuple-element.330) | copy-start | bytes 98308
  105.3 62.4 %copy-start.22 = (f32[1024]{0:T(1024)}, f32[1024]{0:T(1024)S(1)}, u32[]{:S(2)}) copy-start(f32[1024]{0:T(1024)S(1)} %broadcast_multiply_fusion.1) | copy-start | bytes 12292
  107.6 60.1 %copy-start.27 = (f32[1024]{0:T(1024)}, f32[1024]{0:T(1024)S(1)}, u32[]{:S(2)}) copy-start(f32[1024]{0:T(1024)S(1)} %add_rsqrt_fusion) | copy-start | bytes 12292
  175.7 2.8 copy-start.12
  175.7 2.8 copy-start.14
  244.5 21.7 %copy-start = (f32[1024,8,64]{0,2,1:T(8,128)S(1)}, f32[1024,8,64]{0,2,1:T(8,128)}, u32[]{:S(2)}) copy-start(f32[1024,8,64]{0,2,1:T(8,128)} %get-tuple-element.522) | copy-start | bytes 6291460 | tf_op jit(solution)/shard_map/while
  266.2 5.6 copy-start.3
  271.8 9.4 copy-start.1
  314.6 21.7 %copy-start = (f32[1024,8,64]{0,2,1:T(8,128)S(1)}, f32[1024,8,64]{0,2,1:T(8,128)}, u32[]{:S(2)}) copy-start(f32[1024,8,64]{0,2,1:T(8,128)} %get-tuple-element.522) | copy-start | bytes 6291460 | tf_op jit(solution)/shard_map/while
  336.3 5.4 copy-start.3
  341.7 10.0 copy-start.1
  351.7 5.9 copy-start.2
  351.7 6.0 copy-start.16
  351.7 6.0 copy-start.17
  360.2 5.1 copy-start.7
  364.8 2.2 copy-start.8
  367.0 8.2 copy-start.6
  367.1 8.1 copy-start.21
  367.1 8.1 copy-start.23
  367.1 8.1 copy-start.24
  367.1 8.1 copy-start.28
  367.1 120.0 %reduce-scatter.27.cloned.1.call-start = ((), (), s32[]{:S(2)}) async-start(), calls=%async_computation.21 | async-start | bytes 1114112
  375.2 9.3 copy-start.18
  413.9 168.3 %reduce-scatter.15.cloned.1.call-start = ((), (), s32[]{:S(2)}) async-start(), calls=%async_computation.15 | async-start | bytes 12582912 | tf_op jit(solution)/shard_map/reduce_scatter | solution.py:205
  413.9 7.8 copy-start.10
  425.8 212.9 %reduce-scatter.13.cloned.1.call-start = ((), (), s32[]{:S(2)}) async-start(), calls=%async_computation.13 | async-start | bytes 6291456 | tf_op jit(solution)/shard_map/reduce_scatter | solution.py:136
  428.8 18.5 %copy-start.9 = (bf16[64,8,2,512]{3,1,2,0:T(8,128)(2,1)}, bf16[64,8,2,512]{3,1,2,0:T(8,128)(2,1)S(1)}, u32[]{:S(2)}) copy-start(bf16[64,8,2,512]{3,1,2,0:T(8,128)(2,1)S(1)} %copy.85) | copy-start | bytes 3145732
  439.5 7.8 copy-start.11
  450.6 4.8 copy-start.20
  450.7 4.8 copy-start.26
  450.7 254.5 %reduce-scatter.19.cloned.1.call-start = ((), (), s32[]{:S(2)}) async-start(), calls=%async_computation.17 | async-start | bytes 2228224 | tf_op jit(solution)/shard_map/reduce_scatter | solution.py:234
  455.4 338.4 %reduce-scatter.17.cloned.1.call-start = ((), (), s32[]{:S(2)}) async-start(), calls=%async_computation.16 | async-start | bytes 6684672 | tf_op jit(solution)/shard_map/reduce_scatter | solution.py:232
  463.4 439.3 %reduce-scatter.23.cloned.1.call-start = ((), (), s32[]{:S(2)}) async-start(), calls=%async_computation.19 | async-start | bytes 8912896 | tf_op jit(solution)/shard_map/reduce_scatter | solution.py:237
  474.3 537.8 %reduce-scatter.21.cloned.1.call-start = ((), (), s32[]{:S(2)}) async-start(), calls=%async_computation.18 | async-start | bytes 8912896 | tf_op jit(solution)/shard_map/reduce_scatter | solution.py:235
  483.7 1.2 copy-start.4
  483.7 1.9 copy-start.29
  483.7 1.9 copy-start.30
  582.2 3.4 copy-start.5
  683.0 329.7 %copy-start.31 = (f32[32]{0:T(128)}, f32[32]{0:T(128)S(1)}, u32[]{:S(2)}) copy-start(f32[32]{0:T(128)S(1)} %dynamic-slice.4) | copy-start | bytes 388
  (1 other events, 1.0 us)
Sparse Core Ops, SparseCore 0:
  9.6 36.5 all-gather.6
  48.3 38.3 all-gather.10
  88.2 32.2 all-gather.16
  122.5 45.2 all-gather.8
  169.8 49.5 all-gather.12
  221.4 49.0 all-gather.14
  367.2 54.1 reduce-scatter.24
  425.0 56.5 reduce-scatter.26
  483.9 98.1 reduce-scatter.14
  584.3 54.2 reduce-scatter.12
  643.4 61.7 reduce-scatter.18
  709.5 84.2 reduce-scatter.16
  799.0 103.6 reduce-scatter.22
  907.8 104.3 reduce-scatter.20
where the time goes:
time: 1030 us; the launch traced here: 1020 us
  waiting for transfers between devices  530 us (51%)
  matrix products  199 us (19%)
  blocking collectives  122 us (12%)
  local copies, waits for them, and re-layouts  83.1 us (8%)
  other arithmetic  68.2 us (7%)
  between operations  14.7 us (1%)
    reduce_scatter x1, waiting for transfers between devices, local(): lax.psum_scatter(unit_sums[0], 'dp', scatter_dimension=0, tiled=True)  109 us
    reduce_scatter x1, waiting for transfers between devices, local(): lax.psum_scatter(unit_sums[2], 'dp', scatter_dimension=1, tiled=True)  109 us
    reduce_scatter x1, waiting for transfers between devices, local(): lax.psum_scatter(jnp.stack([attn_term, mlp_term], axis=1), 'tensor', scat...  93.6 us
    reduce_scatter x1, waiting for transfers between devices, local(): lax.psum_scatter(d_w_qkv, 'dp', scatter_dimension=0, tiled=True)  88.6 us
    unnamed x2, blocking collectives  82.3 us
    reduce_scatter x1, waiting for transfers between devices, local(): lax.psum_scatter(jnp.dot(context_part, w_out, preferred_element_type=jnp....  51.8 us
    dynamic_update_slice x4, local copies, waits for them, and re-layouts, local(): lax.map(forward_block, (query_blocks, segment_blocks, place_blocks))  43.4 us
    all_gather x1, waiting for transfers between devices, local(): lax.all_gather(qkv_weight, 'dp', axis=0, tiled=True)  40.8 us
  transfers between devices with their start and end apart: 14, of which 8 were waited for; matrix products, arithmetic and copies ran while one was open for 34% of the time, Pallas kernels for 0%

commit v1 on v0

--- a/solution.py
+++ b/solution.py
@@ -1,16 +1,709 @@
+import functools
 import math
 
 import jax
 import jax.numpy as jnp
+import numpy as np
 from jax import lax
+from jax.experimental import pallas as pl
+from jax.experimental.pallas import tpu as pltpu
 from jax.sharding import PartitionSpec as P
 
 HEAD = 64
 ROT = 16
 
-
 EPSILON = 1e-05
 NEGATIVE = -1e30
+MESH = pl.DeviceIdType.MESH
+F32 = jnp.float32
+BF16 = jnp.bfloat16
+NN = (((1,), (0,)), ((), ()))
+NT = (((1,), (1,)), ((), ()))
+TN = (((0,), (0,)), ((), ()))
+VMEM_BYTES = 63 << 20
+
+
+def dot(a, b, dims=NN):
+    return lax.dot_general(a, b, dims, preferred_element_type=F32)
+
+
+class Sizes:
+    def __init__(self, n_dp, n_t, seq, rows, d, width, units):
+        self.n_dp, self.n_t, self.seq, self.rows, self.d = n_dp, n_t, seq, rows, d
+        self.width, self.units = width, units
+        self.nz = n_dp // 4
+        self.shard = d // n_dp
+        self.nf = units // width
+        self.chunks = 4 + 2 * self.nf
+        self.block = min(256, rows)
+        self.n_blocks = seq // self.block
+        self.own_blocks = rows // self.block
+        self.pairs = width // 128
+        self.sums_width = max(d, 3 * width, units)
+        self.p_slots = 2
+        self.r_slots = 4
+
+
+def fused_kernel(sz, *refs):
+    (
+        x_hbm, g_hbm, w_hbm, small_in, seg_ref, cos_ref, sin_ref,
+        out_hbm, igrad_hbm, dw_ref, sums_ref,
+        xa, ga, ha, hm, stat, wts, sm, vec_d, vec_q, vec_u, pool, ctx, dproj, dup, acc, bias,
+        part, red_c, red_y, red_z, b_send, b_recv, h_send, h_recv, sums_in,
+        local_sem, sm_s, sm_r, row_s, row_r, gz_s, gz_r, gy_s, gy_r, gc_s, gc_r,
+        rc_s, rc_r, ry_s, ry_r, rz_s, rz_r, xt_s, xt_r, su_s, su_r, credit,
+    ) = refs
+    nz, r, D, W, S, R, T = sz.nz, sz.shard, sz.d, sz.width, sz.seq, sz.rows, sz.n_t
+    nf, NCH = sz.nf, sz.chunks
+    dp = lax.axis_index("dp")
+    t = lax.axis_index("tensor")
+    z, y, c = lax.div(dp, 4), lax.rem(lax.div(dp, 2), 2), lax.rem(dp, 2)
+
+    def dev(z_, y_, c_, t_):
+        return ((z_ * 2 + y_) * 2 + c_, t_)
+
+    z_peer = [dev(lax.rem(z + k, nz), y, c, t) for k in range(1, nz)]
+    y_peer = dev(z, 1 - y, c, t)
+    c_peer = dev(z, y, 1 - c, t)
+    t_peer = [dev(z, y, c, lax.rem(t + k, T)) for k in range(1, T)]
+
+    def remote(src, dst, s_sem, r_sem, to):
+        return pltpu.make_async_remote_copy(
+            src_ref=src, dst_ref=dst, send_sem=s_sem, recv_sem=r_sem, device_id=to, device_id_type=MESH
+        )
+
+    own = pl.ds(pl.multiple_of(t * R, R), R)
+
+    cp_w = pltpu.make_async_copy(w_hbm, wts.at[:, z, y, c], local_sem.at[0])
+    cp_x = pltpu.make_async_copy(x_hbm, xa.at[own], local_sem.at[1])
+    cp_g = pltpu.make_async_copy(g_hbm, ga.at[own], local_sem.at[2])
+    cp_w.start()
+    cp_x.start()
+    cp_g.start()
+    sm[z, y, c, t] = small_in[...]
+    barrier = pltpu.get_barrier_semaphore()
+    everyone = z_peer + [y_peer, c_peer] + t_peer
+    for peer in everyone:
+        pl.semaphore_signal(barrier, inc=1, device_id=peer, device_id_type=MESH)
+    pl.semaphore_wait(barrier, len(everyone))
+
+    sm_t = [remote(sm.at[z, y, c, t], sm.at[z, y, c, t], sm_s.at[k], sm_r.at[k], t_peer[k]) for k in range(T - 1)]
+    for cp in sm_t:
+        cp.start()
+    cp_w.wait()
+
+    def gz(ch, k):
+        return remote(wts.at[ch, z, y, c], wts.at[ch, z, y, c], gz_s.at[ch, k], gz_r.at[ch, k], z_peer[k])
+
+    def gy(ch):
+        return remote(wts.at[ch, :, y, c], wts.at[ch, :, y, c], gy_s.at[ch], gy_r.at[ch], y_peer)
+
+    def gc(ch):
+        return remote(wts.at[ch, :, :, c], wts.at[ch, :, :, c], gc_s.at[ch], gc_r.at[ch], c_peer)
+
+    cp_x.wait()
+    cp_g.wait()
+    row_x = [remote(xa.at[own], xa.at[own], row_s.at[0, k], row_r.at[0, k], t_peer[k]) for k in range(T - 1)]
+    row_g = [remote(ga.at[own], ga.at[own], row_s.at[1, k], row_r.at[1, k], t_peer[k]) for k in range(T - 1)]
+    for cp in row_x:
+        cp.start()
+    sm_z = [remote(sm.at[z, y, c], sm.at[z, y, c], sm_s.at[T - 1 + k], sm_r.at[T - 1 + k], z_peer[k]) for k in range(nz - 1)]
+    sm_y = remote(sm.at[:, y, c], sm.at[:, y, c], sm_s.at[T + nz - 2], sm_r.at[T + nz - 2], y_peer)
+    sm_c = remote(sm.at[:, :, c], sm.at[:, :, c], sm_s.at[T + nz - 1], sm_r.at[T + nz - 1], c_peer)
+    for cp in sm_t:
+        cp.wait_recv()
+    for cp in sm_z:
+        cp.start()
+
+    def start_z(ch, carry):
+        for k in range(nz - 1):
+            gz(ch, k).start()
+        return carry
+
+    lax.fori_loop(0, NCH, start_z, 0)
+    for cp in row_g:
+        cp.start()
+
+    def gather_event(e):
+        def on_y():
+            for k in range(nz - 1):
+                gz(e, k).wait_recv()
+            gy(e).start()
+
+        def on_c():
+            gy(e - 1).wait_recv()
+            gc(e - 1).start()
+
+        if isinstance(e, int):
+            if e < NCH:
+                on_y()
+            if 1 <= e <= NCH:
+                on_c()
+        else:
+            pl.when(e < NCH)(on_y)
+            pl.when((e >= 1) & (e <= NCH))(on_c)
+
+    def weights(ch):
+        return wts[ch].reshape(D, W)
+
+    def weight_rows(ch, i, n):
+        if n <= nz:
+            return wts[ch, pl.ds(i * (nz // n), nz // n)].reshape(D // n, W)
+        return wts[ch].reshape(D, W)
+
+    for cp in sm_z:
+        cp.wait_recv()
+    sm_y.start()
+    tile = 128
+
+    def stat_rows(first, count):
+        def body(i, carry):
+            rows = pl.ds(pl.multiple_of(first + i * tile, tile), tile)
+            v = xa[rows, :].astype(F32)
+            mean = jnp.mean(v, axis=-1, keepdims=True)
+            cen = v - mean
+            inv = lax.rsqrt(jnp.mean(cen * cen, axis=-1, keepdims=True) + EPSILON)
+            stat[0, rows, :] = jnp.broadcast_to(mean, (tile, 128))
+            stat[1, rows, :] = jnp.broadcast_to(inv, (tile, 128))
+            return carry
+
+        lax.fori_loop(0, count // tile, body, 0)
+
+    stat_rows(t * R, R)
+    sm_y.wait_recv()
+    sm_c.start()
+    gather_event(0)
+    sm_c.wait_recv()
+
+    flat = sm[...].reshape(sz.n_dp * T * 16, 128)
+    n_rows = sz.n_dp * T * 16
+    pick = (
+        jnp.bitwise_and(lax.broadcasted_iota(jnp.int32, (16, n_rows), 1), 15)
+        == lax.broadcasted_iota(jnp.int32, (16, n_rows), 0)
+    ).astype(F32).astype(BF16)
+
+    def lay_out(width, n, mine_only):
+        shift = n.bit_length() - 1
+        lane_of = lax.broadcasted_iota(jnp.int32, (128, width), 1)
+        spread = (jnp.bitwise_and(lane_of, n - 1) == lax.broadcasted_iota(jnp.int32, (128, width), 0)).astype(F32).astype(BF16)
+        wide = dot(flat, spread)
+        piece = jnp.right_shift(lax.broadcasted_iota(jnp.int32, (n_rows, width), 1), shift)
+        owner = jnp.right_shift(lax.broadcasted_iota(jnp.int32, (n_rows, width), 0), 4)
+        if mine_only:
+            piece = piece * T + t
+        return dot(pick, jnp.where(piece == owner, wide, 0.0).astype(BF16))
+
+    vec_d[...] = lay_out(D, D // (sz.n_dp * T), False)
+    vec_q[...] = lay_out(W, W // sz.n_dp, True)
+    for f in range(nf):
+        vec_u_part = lay_out_units(sz, flat, pick, n_rows, t, f)
+        vec_u[f] = vec_u_part
+
+    def norm_rows(first, count):
+        def body(i, carry):
+            rows = pl.ds(pl.multiple_of(first + i * tile, tile), tile)
+            norm = (xa[rows, :].astype(F32) - stat[0, rows, 0:1]) * stat[1, rows, 0:1]
+            ha[rows, :] = (norm * vec_d[0:1, :] + vec_d[1:2, :]).astype(BF16)
+            hm[rows, :] = (norm * vec_d[2:3, :] + vec_d[3:4, :]).astype(BF16)
+            return carry
+
+        lax.fori_loop(0, count // tile, body, 0)
+
+    norm_rows(t * R, R)
+    gather_event(1)
+    for k in range(1, T):
+        row_x[k - 1].wait_recv()
+        first = lax.rem(t + T - k, T) * R
+        stat_rows(first, R)
+        norm_rows(first, R)
+
+    lane = lax.broadcasted_iota(jnp.int32, (1, 128), 1)
+    low_half = lane < HEAD
+    from_right = jnp.bitwise_and(lane, HEAD - 1) < ROT // 2
+
+    def turned(u, rows, sign):
+        other = jnp.where(from_right, pltpu.roll(u, 128 - ROT // 2, 1), pltpu.roll(u, ROT // 2, 1))
+        turn = other * sin_ref[rows, :]
+        return u * cos_ref[rows, :] + (turn if sign > 0 else -turn)
+
+    big = min(512, R)
+    for j in range(3):
+        gather_event(j + 2)
+        gc(j).wait_recv()
+
+        def project(i, carry, j=j):
+            rows = pl.ds(pl.multiple_of(i * big, big), big)
+            u = dot(ha[rows, :], weights(j)) + vec_q[6 + j : 7 + j, :]
+            for g in range(sz.pairs):
+                part_u = u[:, g * 128 : (g + 1) * 128]
+                if j < 2:
+                    part_u = turned(part_u, rows, 1)
+                if j == 0:
+                    part_u = part_u * (1.0 / math.sqrt(HEAD))
+                pool[j, rows, g * 128 : (g + 1) * 128] = part_u.astype(BF16)
+            return carry
+
+        lax.fori_loop(0, S // big, project, 0)
+    gc(3).wait_recv()
+
+    def d_context(first):
+        def body(i, carry):
+            rows = pl.ds(pl.multiple_of(first + i * big, big), big)
+            pool[3, rows, :] = dot(ga[rows, :], weights(3)).astype(BF16)
+            return carry
+
+        lax.fori_loop(0, R // big, body, 0)
+
+    d_context(t * R)
+    acc[...] = jnp.zeros_like(acc)
+
+    B = sz.block
+    n_steps = sz.n_blocks * sz.pairs
+    first_event = 5
+    stride = 3
+
+    def attend(qb, step0):
+        L = (qb + 1) * B
+        rows = pl.ds(qb * B, B)
+        for s in range(B // 128):
+            here = pl.ds(s * 128, 128)
+            start = jnp.broadcast_to(seg_ref[0:1, qb * B + s * 128 : qb * B + (s + 1) * 128].astype(F32), (128, 128)).T
+            start = start[:, 0:1].astype(jnp.int32)
+            key_at = lax.broadcasted_iota(jnp.int32, (128, L), 1)
+            row_at = lax.broadcasted_iota(jnp.int32, (128, L), 0) + (qb * B + s * 128)
+            bias[here, :L] = jnp.where((key_at >= start) & (key_at <= row_at), 0.0, NEGATIVE)
+
+        def pair(p, carry):
+            cols = pl.ds(pl.multiple_of(p * 128, 128), 128)
+            keys, values = pool[1, :L, cols], pool[2, :L, cols]
+            query, d_ctx = pool[0, rows, cols], pool[3, rows, cols]
+            made = []
+            for h in range(2):
+                mine = low_half if h == 0 else jnp.logical_not(low_half)
+                q_h = jnp.where(mine, query, jnp.zeros_like(query))
+                d_h = jnp.where(mine, d_ctx, jnp.zeros_like(d_ctx))
+                scores = dot(q_h, keys, NT) + bias[:, :L]
+                top = jnp.max(scores, axis=1, keepdims=True)
+                e = jnp.exp(scores - top)
+                prob = e * (1.0 / jnp.sum(e, axis=1, keepdims=True))
+                d_prob = dot(d_h, values, NT)
+                delta = jnp.sum(prob * d_prob, axis=1, keepdims=True)
+                d_s = (prob * (d_prob - delta)).astype(BF16)
+                p_b = prob.astype(BF16)
+                made.append((dot(p_b, values), dot(d_s, keys), dot(d_s, q_h, TN), dot(p_b, d_h, TN)))
+            ctx[rows, cols] = jnp.where(low_half, made[0][0], made[1][0]).astype(BF16)
+            d_q = jnp.where(low_half, made[0][1], made[1][1]) * (1.0 / math.sqrt(HEAD))
+            dproj[0, rows, cols] = turned(d_q, rows, -1).astype(BF16)
+            acc[:L, cols] += made[0][2] + made[1][2]
+            cols_v = pl.ds(pl.multiple_of(W + p * 128, 128), 128)
+            acc[:L, cols_v] += made[0][3] + made[1][3]
+            at = step0 + p
+            pl.when(lax.rem(at, stride) == stride - 1)(lambda: gather_event(first_event + lax.div(at, stride)))
+            return carry
+
+        lax.fori_loop(0, sz.pairs, pair, 0)
+
+    def block_step(j, carry):
+        def rest():
+            for k in range(1, T):
+                row_g[k - 1].wait_recv()
+                d_context(lax.rem(t + T - k, T) * R)
+
+        pl.when(j == sz.own_blocks)(rest)
+        which = lax.rem(j + t * sz.own_blocks, sz.n_blocks)
+        for qb in range(sz.n_blocks):
+            pl.when(which == qb)(functools.partial(attend, qb, j * sz.pairs))
+        return carry
+
+    lax.fori_loop(0, sz.n_blocks, block_step, 0)
+    next_event = first_event + n_steps // stride
+
+    def finish_proj(i, carry):
+        rows = pl.ds(pl.multiple_of(i * tile, tile), tile)
+        for g in range(sz.pairs):
+            cols = pl.ds(g * 128, 128)
+            dproj[1, rows, cols] = turned(acc[rows, cols], rows, -1).astype(BF16)
+            dproj[2, rows, cols] = acc[rows, pl.ds(W + g * 128, 128)].astype(BF16)
+        return carry
+
+    lax.fori_loop(0, S // tile, finish_proj, 0)
+
+    def rc(i):
+        return remote(
+            part.at[lax.rem(i, sz.p_slots), :, :, 1 - c], red_c.at[lax.rem(i, sz.r_slots)], rc_s.at[i], rc_r.at[i], c_peer
+        )
+
+    def ry(i):
+        return remote(red_c.at[lax.rem(i, sz.r_slots), :, 1 - y], red_y.at[i], ry_s.at[i], ry_r.at[i], y_peer)
+
+    def rz(i, k):
+        return remote(red_y.at[i, lax.rem(z + k + 1, nz)], red_z.at[i, k], rz_s.at[i, k], rz_r.at[i, k], z_peer[k])
+
+    def emit(i, left, right):
+        slot = lax.rem(i, sz.p_slots)
+
+        def body(n, carry):
+            cols = pl.ds(pl.multiple_of(n * (D // 2), D // 2), D // 2)
+            made = dot(left[:, cols], right[...], TN)
+            part[slot, pl.ds(n * (nz // 2), nz // 2)] = made.astype(BF16).reshape(nz // 2, 2, 2, r, W)
+            return carry
+
+        lax.fori_loop(0, 2, body, 0)
+        pl.when(i >= sz.r_slots)(lambda: pl.semaphore_wait(credit, 1))
+        rc(i).start()
+
+    def event_c(i):
+        rc(i).wait()
+        slot, rslot = lax.rem(i, sz.p_slots), lax.rem(i, sz.r_slots)
+        red_c[rslot] = (part[slot, :, :, c].astype(F32) + red_c[rslot].astype(F32)).astype(BF16)
+        ry(i).start()
+
+    def event_y(i):
+        ry(i).wait()
+        rslot = lax.rem(i, sz.r_slots)
+        red_y[i] = (red_c[rslot, :, y].astype(F32) + red_y[i].astype(F32)).astype(BF16)
+        pl.when(i < NCH - sz.r_slots)(lambda: pl.semaphore_signal(credit, inc=1, device_id=c_peer, device_id_type=MESH))
+        for k in range(nz - 1):
+            rz(i, k).start()
+
+    def event_z(i):
+        for k in range(nz - 1):
+            rz(i, k).wait()
+        total = red_y[i, z].astype(F32)
+        for k in range(nz - 1):
+            total = total + red_z[i, k].astype(F32)
+        dw_ref[i] = total
+
+    sums_ref[...] = jnp.zeros_like(sums_ref)
+
+    def row_sum(v):
+        return jnp.sum(v.astype(F32), axis=0, keepdims=True)
+
+    for j in range(3):
+        emit(j, ha, dproj.at[j])
+        sums_ref[5:6, j * W : (j + 1) * W] = row_sum(dproj[j])
+        if j:
+            event_c(j - 1)
+    emit(3, ga, ctx)
+    event_c(2)
+    for e in range(next_event, NCH + 1):
+        gather_event(e)
+    event_c(3)
+
+    for ch in range(4, NCH):
+        gc(ch).wait_recv()
+
+    def mlp(first, f):
+        def body(i, carry):
+            rows = pl.ds(pl.multiple_of(first + i * big, big), big)
+            u = dot(hm[rows, :], weights(4 + 2 * f)) + vec_u[f, 9:10, :]
+            cdf = 0.5 + 0.5 * lax.erf(u * math.sqrt(0.5))
+            pool[f, rows, :] = (u * cdf).astype(BF16)
+            slope = cdf + u * (jnp.exp(u * u * -0.5) * (1.0 / math.sqrt(2.0 * math.pi)))
+            back = slope * dot(ga[rows, :], weights(5 + 2 * f))
+            dup[f, rows, :] = back.astype(BF16)
+            return carry
+
+        lax.fori_loop(0, R // big, body, 0)
+
+    half = D // 2
+
+    def branch(first, i, n):
+        rows = pl.ds(pl.multiple_of(first + i * big, big), big)
+        total = dot(ctx[rows, :], weight_rows(3, n, 2), NT)
+        for f in range(nf):
+            total = total + dot(pool[f, rows, :], weight_rows(5 + 2 * f, n, 2), NT)
+        return total
+
+    def d_hidden(first, i, n):
+        rows = pl.ds(pl.multiple_of(first + i * big, big), big)
+        cols = pl.ds(pl.multiple_of(n * half, half), half)
+        d_attn = dot(dproj[0, rows, :], weight_rows(0, n, 2), NT)
+        for j in range(1, 3):
+            d_attn = d_attn + dot(dproj[j, rows, :], weight_rows(j, n, 2), NT)
+        d_mlp = dot(dup[0, rows, :], weight_rows(4, n, 2), NT)
+        for f in range(1, nf):
+            d_mlp = d_mlp + dot(dup[f, rows, :], weight_rows(4 + 2 * f, n, 2), NT)
+        norm = (xa[rows, cols].astype(F32) - stat[0, rows, 0:1]) * stat[1, rows, 0:1]
+        sums_ref[0:1, cols] += row_sum(d_attn * norm)
+        sums_ref[1:2, cols] += row_sum(d_attn)
+        sums_ref[2:3, cols] += row_sum(d_mlp * norm)
+        sums_ref[3:4, cols] += row_sum(d_mlp)
+        return d_attn * vec_d[0:1, cols] + d_mlp * vec_d[2:3, cols]
+
+    def xt(which, k):
+        src, dst = ((b_send, b_recv), (h_send, h_recv))[which]
+        return remote(src.at[k], dst.at[k], xt_s.at[which, k], xt_r.at[which, k], t_peer[k])
+
+    for k in range(T - 1):
+        first = lax.rem(t + k + 1, T) * R
+
+        def forward_units(f, carry, first=first):
+            mlp(first, f)
+            return carry
+
+        lax.fori_loop(0, nf, forward_units, 0)
+        if k == 0:
+            event_y(0)
+
+        def both(q, carry, first=first, k=k):
+            i, n = lax.div(q, 2), lax.rem(q, 2)
+            cols = pl.ds(pl.multiple_of(n * half, half), half)
+            rows = pl.ds(pl.multiple_of(i * big, big), big)
+            b_send[k, rows, cols] = branch(first, i, n).astype(BF16)
+            return carry
+
+        lax.fori_loop(0, 2 * (R // big), both, 0)
+        xt(0, k).start()
+        if k == 0:
+            event_y(1)
+            event_z(0)
+
+        def both_back(q, carry, first=first, k=k):
+            i, n = lax.div(q, 2), lax.rem(q, 2)
+            cols = pl.ds(pl.multiple_of(n * half, half), half)
+            rows = pl.ds(pl.multiple_of(i * big, big), big)
+            h_send[k, rows, cols] = d_hidden(first, i, n).astype(BF16)
+            return carry
+
+        lax.fori_loop(0, 2 * (R // big), both_back, 0)
+        xt(1, k).start()
+
+    def own_units(f, carry):
+        mlp(t * R, f)
+        first = 4 + 2 * f
+        sums_ref[6:7, pl.ds(pl.multiple_of(f * W, W), W)] = row_sum(dup[f])
+        emit(first, hm, dup.at[f])
+        pl.when(f > 0)(lambda: event_c(first - 1))
+        event_y(first - 2)
+        event_z(first - 3)
+        emit(first + 1, ga, pool.at[f])
+        event_c(first)
+        event_y(first - 1)
+        event_z(first - 2)
+        return carry
+
+    lax.fori_loop(0, nf, own_units, 0)
+    last = NCH - 1
+    event_c(last)
+
+    def own_both(q, carry):
+        i, n = lax.div(q, 2), lax.rem(q, 2)
+        cols = pl.ds(pl.multiple_of(n * half, half), half)
+        acc[pl.ds(pl.multiple_of(i * big, big), big), cols] = branch(t * R, i, n)
+        return carry
+
+    lax.fori_loop(0, 2 * (R // big), own_both, 0)
+    event_y(last - 1)
+    event_z(last - 2)
+
+    def own_back(q, carry):
+        i, n = lax.div(q, 2), lax.rem(q, 2)
+        cols = pl.ds(pl.multiple_of(n * half, half), half)
+        acc[pl.ds(pl.multiple_of(R + i * big, big), big), cols] = d_hidden(t * R, i, n)
+        return carry
+
+    lax.fori_loop(0, 2 * (R // big), own_back, 0)
+    sums_ref[4:5, :D] = row_sum(ga[own, :])
+    event_y(last)
+
+    su_c = remote(sums_ref, sums_in.at[0], su_s.at[0], su_r.at[0], c_peer)
+    su_c.start()
+    event_z(last - 1)
+    su_c.wait()
+    sums_ref[...] += sums_in[0]
+    su_y = remote(sums_ref, sums_in.at[1], su_s.at[1], su_r.at[1], y_peer)
+    su_y.start()
+
+    for k in range(T - 1):
+        xt(0, k).wait()
+
+    def finish_out(i, carry):
+        rows = pl.ds(pl.multiple_of(i * tile, tile), tile)
+        here = pl.ds(pl.multiple_of(t * R + i * tile, tile), tile)
+        total = xa[here, :].astype(F32) + acc[rows, :] + (vec_d[4:5, :] + vec_d[5:6, :])
+        for k in range(T - 1):
+            total = total + b_recv[k, rows, :].astype(F32)
+        b_send[0, rows, :] = total.astype(BF16)
+        return carry
+
+    lax.fori_loop(0, R // tile, finish_out, 0)
+    cp_out = pltpu.make_async_copy(b_send.at[0], out_hbm, local_sem.at[3])
+    cp_out.start()
+    su_y.wait()
+    sums_ref[...] += sums_in[1]
+    su_z = [remote(sums_ref, sums_in.at[2 + k], su_s.at[2 + k], su_r.at[2 + k], z_peer[k]) for k in range(nz - 1)]
+    for cp in su_z:
+        cp.start()
+
+    for k in range(T - 1):
+        xt(1, k).wait()
+
+    def finish_grad(i, carry):
+        rows = pl.ds(pl.multiple_of(R + i * tile, tile), tile)
+        there = pl.ds(pl.multiple_of(i * tile, tile), tile)
+        here = pl.ds(pl.multiple_of(t * R + i * tile, tile), tile)
+        inv = stat[1, here, 0:1]
+        norm = (xa[here, :].astype(F32) - stat[0, here, 0:1]) * inv
+        d_hat = acc[rows, :]
+        for k in range(T - 1):
+            d_hat = d_hat + h_recv[k, there, :].astype(F32)
+        inner = jnp.mean(d_hat * norm, axis=-1, keepdims=True)
+        acc[rows, :] = ga[here, :].astype(F32) + inv * (d_hat - jnp.mean(d_hat, axis=-1, keepdims=True) - norm * inner)
+        return carry
+
+    lax.fori_loop(0, R // tile, finish_grad, 0)
+    cp_grad = pltpu.make_async_copy(acc.at[pl.ds(R, R)], igrad_hbm, local_sem.at[4])
+    cp_grad.start()
+    for cp in su_z:
+        cp.wait()
+    for k in range(nz - 1):
+        sums_ref[...] += sums_in[2 + k]
+    su_t = [
+        remote(sums_ref, sums_in.at[1 + nz + k], su_s.at[1 + nz + k], su_r.at[1 + nz + k], t_peer[k]) for k in range(T - 1)
+    ]
+    for cp in su_t:
+        cp.start()
+    event_z(last)
+    for cp in su_t:
+        cp.wait()
+    for k in range(T - 1):
+        sums_ref[0:5, :] += sums_in[1 + nz + k, 0:5, :]
+
+    for cp in sm_t + sm_z + [sm_y, sm_c] + row_x + row_g:
+        cp.wait_send()
+
+    def sent(ch, carry):
+        for k in range(nz - 1):
+            gz(ch, k).wait_send()
+        gy(ch).wait_send()
+        gc(ch).wait_send()
+        return carry
+
+    lax.fori_loop(0, NCH, sent, 0)
+    cp_out.wait()
+    cp_grad.wait()
+
+
+def lay_out_units(sz, flat, pick, n_rows, t, f):
+    n = sz.units // sz.n_dp
+    shift = n.bit_length() - 1
+    W = sz.width
+    lane_of = lax.broadcasted_iota(jnp.int32, (128, W), 1) + f * W
+    spread = (jnp.bitwise_and(lane_of, n - 1) == lax.broadcasted_iota(jnp.int32, (128, W), 0)).astype(F32).astype(BF16)
+    wide = dot(flat, spread)
+    piece = jnp.right_shift(lax.broadcasted_iota(jnp.int32, (n_rows, W), 1) + f * W, shift) * sz.n_t + t
+    owner = jnp.right_shift(lax.broadcasted_iota(jnp.int32, (n_rows, W), 0), 4)
+    return dot(pick, jnp.where(piece == owner, wide, 0.0).astype(BF16))
+
+
+def fused(sz, args):
+    (
+        inputs, segment_ids, ln_attn_gain, ln_attn_bias, ln_mlp_gain, ln_mlp_bias, qkv_weight, qkv_bias,
+        out_weight, out_bias, up_weight, up_bias, down_weight, down_bias, cotangent,
+    ) = args
+    nz, r, D, W, S, R, T, nf, NCH = sz.nz, sz.shard, sz.d, sz.width, sz.seq, sz.rows, sz.n_t, sz.nf, sz.chunks
+
+    def row(v):
+        v = v.reshape(1, -1)
+        return jnp.pad(v, ((0, 0), (0, 128 - v.shape[1])))
+
+    small = jnp.concatenate(
+        [row(v) for v in (ln_attn_gain, ln_attn_bias, ln_mlp_gain, ln_mlp_bias, out_bias, down_bias)]
+        + [row(qkv_bias[j]) for j in range(3)]
+        + [row(up_bias), jnp.zeros((6, 128), BF16)],
+        axis=0,
+    )
+    up = up_weight.reshape(r, nf, W).transpose(1, 0, 2)
+    down = down_weight.reshape(nf, W, r).transpose(0, 2, 1)
+    packed = jnp.concatenate(
+        [
+            qkv_weight.transpose(1, 0, 2),
+            out_weight.T[None],
+            jnp.stack([up, down], axis=1).reshape(2 * nf, r, W),
+        ],
+        axis=0,
+    )
+    half_rot = ROT // 2
+    place = np.arange(S, dtype=np.float32)
+    inverse = (10000.0 ** (-(2.0 * np.arange(half_rot, dtype=np.float32)) / ROT)).astype(np.float32)
+    theta = place[:, None] * inverse[None, :]
+    cos, sin = np.cos(theta), np.sin(theta)
+    cos_head = np.concatenate([cos, cos, np.ones((S, HEAD - ROT), np.float32)], axis=1)
+    sin_head = np.concatenate([-sin, sin, np.zeros((S, HEAD - ROT), np.float32)], axis=1)
+    cos_table = jnp.asarray(np.tile(cos_head, (1, 128 // HEAD)), F32)
+    sin_table = jnp.asarray(np.tile(sin_head, (1, 128 // HEAD)), F32)
+
+    hbm = pl.BlockSpec(memory_space=pl.ANY)
+    vmem = pl.BlockSpec(memory_space=pltpu.VMEM)
+    sw = sz.sums_width
+    dma = pltpu.SemaphoreType.DMA
+    n_small = T - 1 + nz - 1 + 2
+    scratch = [
+        pltpu.VMEM((S, D), BF16),
+        pltpu.VMEM((S, D), BF16),
+        pltpu.VMEM((S, D), BF16),
+        pltpu.VMEM((S, D), BF16),
+        pltpu.VMEM((2, S, 128), F32),
+        pltpu.VMEM((NCH, nz, 2, 2, r, W), BF16),
+        pltpu.VMEM((nz, 2, 2, T, 16, 128), BF16),
+        pltpu.VMEM((16, D), F32),
+        pltpu.VMEM((16, W), F32),
+        pltpu.VMEM((nf, 16, W), F32),
+        pltpu.VMEM((max(4, nf), S, W), BF16),
+        pltpu.VMEM((S, W), BF16),
+        pltpu.VMEM((3, S, W), BF16),
+        pltpu.VMEM((nf, S, W), BF16),
+        pltpu.VMEM((S, D), F32),
+        pltpu.VMEM((sz.block, S), F32),
+        pltpu.VMEM((sz.p_slots, nz, 2, 2, r, W), BF16),
+        pltpu.VMEM((sz.r_slots, nz, 2, r, W), BF16),
+        pltpu.VMEM((NCH, nz, r, W), BF16),
+        pltpu.VMEM((NCH, nz - 1, r, W), BF16),
+        pltpu.VMEM((T - 1, R, D), BF16),
+        pltpu.VMEM((T - 1, R, D), BF16),
+        pltpu.VMEM((T - 1, R, D), BF16),
+        pltpu.VMEM((T - 1, R, D), BF16),
+        pltpu.VMEM((nz + T, 8, sw), F32),
+        dma((5,)),
+        dma((n_small,)), dma((n_small,)),
+        dma((2, T - 1)), dma((2, T - 1)),
+        dma((NCH, nz - 1)), dma((NCH, nz - 1)),
+        dma((NCH,)), dma((NCH,)),
+        dma((NCH,)), dma((NCH,)),
+        dma((NCH,)), dma((NCH,)),
+        dma((NCH,)), dma((NCH,)),
+        dma((NCH, nz - 1)), dma((NCH, nz - 1)),
+        dma((2, T - 1)), dma((2, T - 1)),
+        dma((nz + T,)), dma((nz + T,)),
+        pltpu.SemaphoreType.REGULAR,
+    ]
+    output, input_grad, dw, sums = pl.pallas_call(
+        functools.partial(fused_kernel, sz),
+        out_shape=(
+            jax.ShapeDtypeStruct((R, D), BF16),
+            jax.ShapeDtypeStruct((R, D), F32),
+            jax.ShapeDtypeStruct((NCH, r, W), F32),
+            jax.ShapeDtypeStruct((8, sw), F32),
+        ),
+        in_specs=[hbm, hbm, hbm, vmem, vmem, vmem, vmem],
+        out_specs=(hbm, hbm, vmem, vmem),
+        scratch_shapes=scratch,
+        compiler_params=pltpu.CompilerParams(collective_id=0, has_side_effects=True, vmem_limit_bytes=VMEM_BYTES),
+    )(inputs, cotangent, packed, small, segment_ids.reshape(1, S), cos_table, sin_table)
+
+    dp, t = lax.axis_index("dp"), lax.axis_index("tensor")
+    n = D // (sz.n_dp * T)
+    here = lax.dynamic_slice(sums, (0, (dp * T + t) * n), (5, n))
+    nq, nu = W // sz.n_dp, sz.units // sz.n_dp
+    d_qkv_bias = lax.dynamic_slice(sums[5, : 3 * W].reshape(3, 1, W), (0, 0, dp * nq), (3, 1, nq))
+    d_up_bias = lax.dynamic_slice(sums, (6, dp * nu), (1, nu))
+    return (
+        output, input_grad, here[0], here[1], here[2], here[3],
+        dw[:3].transpose(1, 0, 2), d_qkv_bias, dw[3].T, here[4],
+        dw[4::2].transpose(1, 0, 2).reshape(r, sz.units), d_up_bias,
+        dw[5::2].transpose(0, 2, 1).reshape(sz.units, r), here[4],
+    )
 
 
 def rotated(values, cosine, sine, sign):
@@ -39,7 +732,7 @@
     return (centred * inv_std, inv_std)
 
 
-def local(
+def plain(
     inputs,
     segment_ids,
     ln_attn_gain,
@@ -254,9 +947,31 @@
     )
 
 
+def fits(n_dp, n_t, seq, rows, d, width, units):
+    if n_dp % 8 or n_t < 2 or width % 128 or units % width or rows % 128 or seq != rows * n_t:
+        return False
+    small = (d // (n_dp * n_t), width // n_dp, units // n_dp)
+    if any(n < 1 or n > 128 or n & (n - 1) for n in small) or (d // n_dp) % 16:
+        return False
+    rows_of = 2 * (4 * seq * d + seq * (max(4, units // width) * width + 4 * width + units)) + 4 * seq * d
+    chunks = 4 + 2 * (units // width)
+    weights_of = 2 * chunks * d * width
+    reduction = 2 * d * width * (2 + 2) + weights_of * 7 // 16 + 4 * chunks * (d // n_dp) * width
+    exchange = 8 * (n_t - 1) * rows * d
+    return rows_of + weights_of + reduction + exchange <= 54 << 20
+
+
+def local(n_dp, n_t, *args):
+    rows, d = args[0].shape
+    seq, width, units = args[1].shape[0], args[6].shape[2], args[10].shape[1]
+    if fits(n_dp, n_t, seq, rows, d, width, units):
+        return fused(Sizes(n_dp, n_t, seq, rows, d, width, units), args)
+    return plain(*args)
+
+
 def solution(mesh):
     return jax.shard_map(
-        local,
+        functools.partial(local, mesh.shape["dp"], mesh.shape["tensor"]),
         mesh=mesh,
         in_specs=(
             P(("dp", "tensor"), None),

time: 1030 us -> 249 us (0.24)
  waiting for transfers between devices: 530 us -> 0 us
  Pallas kernels: 0 us -> 225 us
  matrix products: 199 us -> 0 us
  blocking collectives: 122 us -> 0 us
  other arithmetic: 68.2 us -> 1 us
  local copies, waits for them, and re-layouts: 83.1 us -> 20.9 us
  between operations: 14.7 us -> 0.76 us
    reduce_scatter x6 -> x0, waiting for transfers between devices: 472 us -> none  [the longest x1 109 us: local(): lax.psum_scatter(unit_sums[0], 'dp', scatter_dimension=0, tiled=True)]
    pallas_call x0 -> x1, Pallas kernels: none -> 225 us  [fused(): pl.pallas_call(functools.partial(fused_kernel, sz), out_shape=(jax.ShapeD...]
    dot_general x26 -> x0, matrix products: 199 us -> none  [the longest x4 31.3 us: masked_scores(): jnp.einsum('qhe,khe->hqk', query_part, keys, preferred_element_type=jnp.f...]
    unnamed x2 -> x0, blocking collectives: 82.3 us -> none
    all_gather x6 -> x0, waiting for transfers between devices: 53.6 us -> none  [the longest x1 40.8 us: local(): lax.all_gather(qkv_weight, 'dp', axis=0, tiled=True)]
    dynamic_update_slice x4 -> x0, local copies, waits for them, and re-layouts: 43.4 us -> none  [local(): lax.map(forward_block, (query_blocks, segment_blocks, place_blocks))]
    all_gather x2 -> x0, blocking collectives: 40.1 us -> none  [the longest x1 22.6 us: local(): lax.all_gather(qkv_bias, 'dp', axis=2, tiled=True)]
    convert_element_type x8 -> x0, other arithmetic: 30.5 us -> none  [the longest x2 18.6 us: backward_block(): d_scores = (probability * (d_prob - row_delta)).astype(jnp.bfloat16)]
  transfers between devices with their start and end apart: 14 -> 0, of which waited for: 8 -> 0; matrix products, arithmetic and copies ran while one was open for 34% -> 0% of each run, Pallas kernels for 0% -> 0%
where the time goes in v1:
time: 249 us; the launch traced here: 248 us
  Pallas kernels  225 us (90%)
  local copies, waits for them, and re-layouts  20.9 us (8%)
    pallas_call x1, Pallas kernels, fused(): pl.pallas_call(functools.partial(fused_kernel, sz), out_shape=(jax.ShapeD...  225 us

profile of v1, /device:TPU:0, one launch (start us, length us, event | category | flops | bytes accessed | tf_op | source)
XLA Modules:
  0.0 248.1 jit_solution(48496176146814253)
XLA Ops:
  0.6 0.0 copy-start.3
  0.7 0.0 copy-start.2
  0.7 0.7 pad.28
  1.4 0.7 pad.29
  2.0 0.7 pad.30
  2.7 0.7 pad.31
  3.4 0.7 pad.32
  4.0 0.7 pad.33
  4.7 0.8 slice_bitcast_fusion.9
  5.5 1.9 concatenate.7.refs_3_
  7.4 1.1 bitcast_bitcast_fusion
  8.5 0.1 pad_maximum_fusion.1
  8.5 0.0 copy-done.3
  8.5 0.0 copy-done.2
  8.5 0.9 pad_maximum_fusion.refs_2_
  9.5 225.5 %shard_map.272 = (bf16[512,1024]{1,0:T(8,128)(2,1)}, f32[512,1024]{1,0:T(8,128)}, f32[12,64,512]{2,1,0:T(8,128)}, f32[8,2048]{1,0:T(8,128)}) custom-call(bf16[512,1024]{1,0:T(8,128)(2,1)} %refs_0_.1, bf16[512,1024]{1,0:T(8,128)(2,1)} %refs_1_.1, bf16[12,64,512]{2,1,0:T(8,128)(2,1)} %pad_maximum_fusion.refs_2_, bf16[16,128]{1,0:T(8,128)(2,1)} %concatenate.7.refs_3_, ...), custom_call_target="tpu_custom_call" | custom-call | tf_op jit(solution)/shard_map/pallas_call | solution.py:681
  235.0 1.3 constant_dynamic-slice_fusion
  236.2 0.8 constant_dynamic-slice_fusion.2
  237.0 0.8 slice_reduce_fusion
  237.8 0.5 slice_bitcast_fusion.4
  238.3 0.0 copy-start.4
  238.4 0.1 constant_dynamic-slice_fusion.1
  238.4 0.6 copy.38
  239.0 1.6 slice_bitcast_fusion.3
  240.6 1.8 slice_bitcast_fusion.2
  242.3 1.3 slice_bitcast_fusion
  243.6 0.0 copy-start.1
  243.6 0.8 copy.42
  244.4 0.0 copy-start
  244.5 0.8 copy.41
  245.3 0.0 copy-done.4
  245.3 0.5 copy.48
  245.8 0.0 copy-done.1
  245.8 1.0 copy.49
  246.8 0.0 copy-done
  246.8 1.3 copy.50
  (5 shorter events, 0.0 us)
Async XLA Ops:
  0.6 7.9 %copy-start.3 = (bf16[512,64]{0,1:T(8,128)(2,1)S(1)}, bf16[512,64]{0,1:T(8,128)(2,1)}, u32[]{:S(2)}) copy-start(bf16[512,64]{0,1:T(8,128)(2,1)} %param.25) | copy-start | bytes 196612
  0.7 7.9 %copy-start.2 = (bf16[64,3,512]{2,0,1:T(8,128)(2,1)S(1)}, bf16[64,3,512]{2,0,1:T(8,128)(2,1)}, u32[]{:S(2)}) copy-start(bf16[64,3,512]{2,0,1:T(8,128)(2,1)} %param.23) | copy-start | bytes 589828
  238.3 6.9 %copy-start.4 = (f32[32]{0:T(128)}, f32[32]{0:T(128)S(1)}, u32[]{:S(2)}) copy-start(f32[32]{0:T(128)S(1)} %get-tuple-element.99) | copy-start | bytes 388
  243.6 2.2 copy-start.1
  244.4 2.3 copy-start
